TPU v7x, 32 devices: a whole 2x2x4 slice. The times are simulated.
32 devices in a mesh: hop: 2 (over x), batch: 16 (over z, y, core).
Axes of the slice: x: 2, y: 2, z: 4, core: 2. Of those that a mesh axis runs over, the one named last changes fastest.
Arguments:
- section_rows: bfloat16 [2, 2048, 2048], P('hop', 'batch'), may hold values from -6 to 6
- weights: bfloat16 [2, 2048, 2048], P('hop'), may hold values from -0.125 to 0.125
- relation_table: bfloat16 [256, 2048], replicated, may hold values from -4 to 4
- relation_ids: int32 [2048], P('batch'), may hold values from 0 to 255
Outputs:
- weight_grad: float32 [2, 2048, 2048], P('hop', 'batch')
- relation_grad: float32 [256, 2048], P(('hop', 'batch'))
- query_grad: bfloat16 [2048, 2048], P('batch')
Inputs may be any that keep to these rules, and one draw needn't show every extreme that they name: `relation_ids`: relation index of each query.
All inputs are finite; a program needn't handle non-finite values.
Results may differ from a plain program's by a relative error of at most 0.0064.
Values may be sent and summed in bfloat16 or wider, within the bound.
No kernel may reach another device: no remote copies, remote signals or barrier semaphores. Data moves between devices by JAX's collectives and lax.ppermute only.
A program may use at most 128 MiB of HBM per device.

v0:
```python
import jax
import jax.numpy as jnp
from jax import lax
from jax.sharding import PartitionSpec as P

MB = 2


def from_behind(block, axis, distance):
    devices = range(lax.axis_size(axis))
    route = [(i - distance, i) for i in devices if i - distance in devices]
    return lax.ppermute(block, axis, route)


def pass_forward(block):
    return from_behind(block, "hop", 1)


def pass_back(block):
    return from_behind(block, "hop", -1)


def add_relations(total, term):
    return total + term


def split_sum(onehot, values):
    head = values.astype(jnp.bfloat16)
    rest = values - head.astype(jnp.float32)
    middle = rest.astype(jnp.bfloat16)
    tail = (rest - middle.astype(jnp.float32)).astype(jnp.bfloat16)
    dims = (((0,), (0,)), ((), ()))
    total = lax.dot_general(onehot, head, dims, preferred_element_type=jnp.float32)
    total = total + lax.dot_general(onehot, middle, dims, preferred_element_type=jnp.float32)
    return total + lax.dot_general(onehot, tail, dims, preferred_element_type=jnp.float32)


def local(section_rows, weights, relation_table, relation_ids):
    rows_dev = section_rows.shape[1]
    per_block = rows_dev // MB
    width = weights.shape[1]
    hidden = weights.shape[2]
    count_rel = relation_table.shape[0]
    half = width // 2
    batch_count = lax.axis_size("batch")
    first = lax.axis_index("hop") == 0
    own_rows = section_rows[0]
    weight = weights[0]
    zeros_q = jnp.zeros((per_block, width), jnp.bfloat16)
    zeros_a = jnp.zeros((per_block, hidden), jnp.bfloat16)
    zeros_rel = jnp.zeros((count_rel, width), jnp.float32)

    def lead(block_index):
        block_rows = lax.dynamic_slice_in_dim(own_rows, block_index * per_block, per_block, 0)
        return lax.dot_general(
            block_rows, weight, (((1,), (1,)), ((), ())), preferred_element_type=jnp.float32
        ).astype(jnp.bfloat16)

    def trail(block_index, query):
        cotangent = lax.dynamic_slice_in_dim(own_rows, block_index * per_block, per_block, 0)
        block_ids = lax.dynamic_slice_in_dim(relation_ids, block_index * per_block, per_block, 0)
        onehot = (block_ids[:, None] == lax.iota(jnp.int32, count_rel)[None, :]).astype(
            jnp.bfloat16
        )
        rel = jnp.dot(onehot, relation_table, preferred_element_type=jnp.float32)
        r_re = rel[:, :half]
        r_im = rel[:, half:]
        qf = query.astype(jnp.float32)
        q_re = qf[:, :half]
        q_im = qf[:, half:]
        mixed = jnp.concatenate(
            [q_re * r_re - q_im * r_im, q_re * r_im + q_im * r_re], axis=1
        ).astype(jnp.bfloat16)
        pre = jnp.dot(mixed, weight, preferred_element_type=jnp.float32)
        sig = jax.nn.sigmoid(pre)
        grad_pre = (cotangent.astype(jnp.float32) * (sig * (1.0 + pre * (1.0 - sig)))).astype(
            jnp.bfloat16
        )
        grad_mixed = lax.dot_general(
            grad_pre, weight, (((1,), (1,)), ((), ())), preferred_element_type=jnp.float32
        )
        gz_re = grad_mixed[:, :half]
        gz_im = grad_mixed[:, half:]
        grad_query = jnp.concatenate(
            [gz_re * r_re + gz_im * r_im, gz_im * r_re - gz_re * r_im], axis=1
        ).astype(jnp.bfloat16)
        grad_rel = jnp.concatenate(
            [gz_re * q_re + gz_im * q_im, gz_im * q_re - gz_re * q_im], axis=1
        )
        rel_term = split_sum(onehot, grad_rel)
        return (grad_query, mixed, grad_pre, rel_term)

    def store(stores, slot, g_back, grad_query, mixed, grad_pre, rel_term):
        left_all, right_all, query_all, rel_total = stores
        block_rows = lax.dynamic_slice_in_dim(own_rows, slot * per_block, per_block, 0)
        left_blk = jnp.where(first, g_back, mixed)
        right_blk = jnp.where(first, block_rows, grad_pre)
        query_blk = jnp.where(first, g_back, grad_query)
        left_all = lax.dynamic_update_slice_in_dim(left_all, left_blk, slot * per_block, 0)
        right_all = lax.dynamic_update_slice_in_dim(right_all, right_blk, slot * per_block, 0)
        query_all = lax.dynamic_update_slice_in_dim(query_all, query_blk, slot * per_block, 0)
        rel_total = add_relations(rel_total, rel_term)
        return (left_all, right_all, query_all, rel_total)

    rel_init = jnp.zeros((count_rel, width), jnp.float32)
    stores = (
        jnp.zeros((rows_dev, width), jnp.bfloat16),
        jnp.zeros((rows_dev, hidden), jnp.bfloat16),
        jnp.zeros((rows_dev, width), jnp.bfloat16),
        rel_init,
    )

    def one_block(block_index, carry):
        sent = lax.cond(first, lambda: lead(block_index), lambda: zeros_q)
        received = pass_forward(sent)
        grad_query, mixed, grad_pre, rel_term = lax.cond(
            first,
            lambda: (zeros_q, zeros_q, zeros_a, zeros_rel),
            lambda: trail(block_index, received),
        )
        g_back = pass_back(grad_query)
        return store(carry, block_index, g_back, grad_query, mixed, grad_pre, rel_term)

    stores = lax.fori_loop(0, MB, one_block, stores)
    left_all, right_all, query_all, rel_total = stores
    rel_shard = lax.psum_scatter(rel_total, ("hop", "batch"), scatter_dimension=0, tiled=True)
    total_rows = rows_dev * batch_count
    relation_grad = rel_shard * jnp.sqrt(jnp.float32(count_rel) / jnp.float32(total_rows))
    full_grad = lax.dot_general(
        left_all, right_all, (((0,), (0,)), ((), ())), preferred_element_type=jnp.float32
    )
    grad_shard = lax.psum_scatter(full_grad, "batch", scatter_dimension=0, tiled=True)
    weight_grad = (grad_shard * (1.0 / jnp.sqrt(jnp.float32(total_rows))))[None]
    return (weight_grad, relation_grad, query_all)


def solution(mesh):
    return jax.shard_map(
        local,
        mesh=mesh,
        in_specs=(P("hop", "batch", None), P("hop", None, None), P(), P("batch")),
        out_specs=(P("hop", "batch", None), P(("hop", "batch"), None), P("batch", None)),
        check_vma=False,
    )
```

profile of v0, /device:TPU:9, one launch (start us, length us, event | category | flops | bytes accessed | tf_op | source)
XLA Modules:
  0.0 400.6 jit_solution(18355680387720729380)
XLA Ops:
  7.2 0.0 reduce-scatter.5.cloned.1.call-start
  7.2 0.8 broadcast.19.clone.1
  8.1 0.8 broadcast.19.clone
  9.0 64.8 %while.20 = (s32[]{:T(128)}, bf16[128,2048]{1,0:T(8,128)(2,1)S(1)}, bf16[128,2048]{1,0:T(8,128)(2,1)}, bf16[128,2048]{1,0:T(8,128)(2,1)}, f32[256,2048]{1,0:T(8,...) while((s32[]{:T(128)}, bf16[128,2048]{1,0:T(8,128)(2,1)S(1)}, ...), condition=%wide.region_5.6_spmd.clone, body=%wide.region_0.5_spmd.clone.sunk | while | flops 1887895552 | bytes 98832664 | solution.py:124
  9.0 0.0 copy-start.2
  9.0 0.0 copy-start.8
  9.0 6.2 %conditional.6 = (bf16[64,2048]{1,0:T(8,128)(2,1)S(1)}) conditional(s32[]{:T(128)} %convert_element_type.75, () %tuple.66, (s32[]{:T(128)}, bf16[128,2048]{1,0:T(8,128)(2,1)}, bf16[2048,2048]{1,0:T(8,128)(2,1)}) %tuple.67), branch_computations={%region_1.0_spmd, %region_2.0_spmd} | conditional | flops 537001984 | bytes 8912954 | solution.py:114
  9.0 6.2 %convolution_convert_fusion = bf16[64,2048]{1,0:T(8,128)(2,1)S(1)} fusion(bf16[2048,2048]{1,0:T(8,128)(2,1)} %get-tuple-element.184, bf16[128,2048]{1,0:T(8,128)(2,1)} %get-tuple-element.182, s32[]{:T(128)S(6)} %select_n.42), kind=kOutput, calls=%fused_computation | convolution fusion | flops 537001984 | bytes 8912900 | tf_op jit(solution)/shard_map/while/body/eval_jaxpr/cond/branch_1_fun/dot_general | solution.py:55
  15.2 1.3 collective-permute-start
  16.6 5.2 %collective-permute-done = bf16[64,2048]{1,0:T(8,128)(2,1)S(1)} collective-permute-done((bf16[64,2048]{1,0:T(8,128)(2,1)S(1)}, bf16[64,2048]{1,0:T(8,128)(2,1)S(1)}, u32[]{:S(2)}, u32[]{:S(2)}) %collective-permute-start) | collective-permute-done | bytes 262176 | tf_op jit(solution)/shard_map/while/body/eval_jaxpr/ppermute | solution.py:12
  21.8 0.3 conditional.7
  21.9 0.2 broadcast.16
  22.1 1.3 collective-permute-start.1
  23.4 0.0 copy-start
  23.5 0.0 copy-start.3
  23.5 0.0 copy-start.6
  23.5 1.6 select_add_fusion.2
  25.1 0.1 select_dynamic-update-slice_fusion.6
  25.2 0.0 copy-start.4
  25.2 16.6 %collective-permute-done.1 = bf16[64,2048]{1,0:T(8,128)(2,1)S(1)} collective-permute-done((bf16[64,2048]{1,0:T(8,128)(2,1)S(1)}, bf16[64,2048]{1,0:T(8,128)(2,1)S(1)}, u32[]{:S(2)}, u32[]{:S(2)}) %collective-permute-start.1) | collective-permute-done | bytes 262176 | tf_op jit(solution)/shard_map/while/body/eval_jaxpr/ppermute | solution.py:12
  41.8 0.1 select_dynamic-update-slice_fusion.5
  41.9 0.0 copy-start.7
  41.9 0.8 copy-done.7
  42.7 6.2 %conditional.6 = (bf16[64,2048]{1,0:T(8,128)(2,1)S(1)}) conditional(s32[]{:T(128)} %convert_element_type.75, () %tuple.66, (s32[]{:T(128)}, bf16[128,2048]{1,0:T(8,128)(2,1)}, bf16[2048,2048]{1,0:T(8,128)(2,1)}) %tuple.67), branch_computations={%region_1.0_spmd, %region_2.0_spmd} | conditional | flops 537001984 | bytes 8912954 | solution.py:114
  42.7 6.2 %convolution_convert_fusion = bf16[64,2048]{1,0:T(8,128)(2,1)S(1)} fusion(bf16[2048,2048]{1,0:T(8,128)(2,1)} %get-tuple-element.184, bf16[128,2048]{1,0:T(8,128)(2,1)} %get-tuple-element.182, s32[]{:T(128)S(6)} %select_n.42), kind=kOutput, calls=%fused_computation | convolution fusion | flops 537001984 | bytes 8912900 | tf_op jit(solution)/shard_map/while/body/eval_jaxpr/cond/branch_1_fun/dot_general | solution.py:55
  48.9 1.3 collective-permute-start
  50.2 4.0 collective-permute-done
  54.2 0.3 conditional.7
  54.3 0.2 broadcast.16
  54.5 1.3 collective-permute-start.1
  55.8 0.0 copy-start
  55.8 0.0 copy-start.3
  55.8 0.0 copy-start.6
  55.8 3.3 select_add_fusion.2
  59.2 0.1 select_dynamic-update-slice_fusion.6
  59.3 13.6 %collective-permute-done.1 = bf16[64,2048]{1,0:T(8,128)(2,1)S(1)} collective-permute-done((bf16[64,2048]{1,0:T(8,128)(2,1)S(1)}, bf16[64,2048]{1,0:T(8,128)(2,1)S(1)}, u32[]{:S(2)}, u32[]{:S(2)}) %collective-permute-start.1) | collective-permute-done | bytes 262176 | tf_op jit(solution)/shard_map/while/body/eval_jaxpr/ppermute | solution.py:12
  72.8 0.1 select_dynamic-update-slice_fusion.5
  72.9 0.0 copy-start.7
  73.0 0.8 copy-done.7
  73.7 0.0 reduce-scatter.5.cloned.1.call-update
  73.8 0.0 reduce-scatter.3.cloned.1.call-start
  73.8 1.0 copy-done.5
  74.8 8.1 %fusion.17 = f32[2048,2048]{1,0:T(8,128)} fusion(bf16[128,2048]{1,0:T(8,128)(2,1)S(1)} %get-tuple-element.213, bf16[128,2048]{1,0:T(8,128)(2,1)S(1)} %copy-done.5), kind=kOutput, calls=%fused_computation.36 | convolution fusion | flops 1073741824 | bytes 17825792 | tf_op jit(solution)/shard_map/dot_general | solution.py:129
  82.9 0.0 reduce-scatter.3.cloned.1.call-update
  82.9 115.2 %reduce-scatter.5.cloned.1.call-done = f32[8,2048]{1,0:T(8,128)} async-done(((f32[256,2048]{1,0:T(8,128)}), f32[8,2048]{1,0:T(8,128)}) %reduce-scatter.5.cloned.1.call-update) | async-done | bytes 65552 | tf_op jit(solution)/shard_map/reduce_scatter | solution.py:126
  198.1 1.5 broadcast_multiply_fusion
  199.6 191.8 %reduce-scatter.3.cloned.1.call-done = f32[128,2048]{1,0:T(8,128)} async-done(((f32[2048,2048]{1,0:T(8,128)}), f32[128,2048]{1,0:T(8,128)}) %reduce-scatter.3.cloned.1.call-update) | async-done | bytes 1048592 | tf_op jit(solution)/shard_map/reduce_scatter | solution.py:132
  391.4 2.3 multiply_bitcast_fusion
  (24 shorter events, 0.2 us)
Async XLA Ops:
  7.2 191.0 %reduce-scatter.5.cloned.1.call-start = ((), (), s32[]{:S(2)}) async-start(), calls=%async_computation.3 | async-start | bytes 2162688 | tf_op jit(solution)/shard_map/reduce_scatter | solution.py:126
  9.0 12.8 %copy-start.2 = (bf16[256,2048]{1,0:T(8,128)(2,1)S(1)}, bf16[256,2048]{1,0:T(8,128)(2,1)}, u32[]{:S(2)}) copy-start(bf16[256,2048]{1,0:T(8,128)(2,1)} %get-tuple-element.402) | copy-start | bytes 3145732 | tf_op jit(solution)/shard_map/while
  9.0 12.8 %copy-start.8 = (s32[128]{0:T(128)S(1)}, s32[128]{0:T(128)}, u32[]{:S(2)}) copy-start(s32[128]{0:T(128)} %get-tuple-element.401) | copy-start | bytes 1540 | tf_op jit(solution)/shard_map/while
  15.2 6.6 %collective-permute-start = (bf16[64,2048]{1,0:T(8,128)(2,1)S(1)}, bf16[64,2048]{1,0:T(8,128)(2,1)S(1)}, u32[]{:S(2)}, u32[]{:S(2)}) collective-permute-start(bf16[64,2048]{1,0:T(8,128)(2,1)S(1)} %get-tuple-element.407), channel_id=1, source_target_pairs={{0,16},{1,17},{2,18},{3,19},{4,20},{5,21},{6,22},{7,23},{8,24},{9,... | collective-permute-start | bytes 786440 | tf_op jit(solution)/shard_map/while/body/eval_jaxpr/ppermute | solution.py:12
  22.1 19.6 %collective-permute-start.1 = (bf16[64,2048]{1,0:T(8,128)(2,1)S(1)}, bf16[64,2048]{1,0:T(8,128)(2,1)S(1)}, u32[]{:S(2)}, u32[]{:S(2)}) collective-permute-start(bf16[64,2048]{1,0:T(8,128)(2,1)S(1)} %get-tuple-element.351), channel_id=1, source_target_pairs={{16,0},{17,1},{18,2},{19,3},{20,4},{21,5},{22,6},{23,7},{24,8},{25... | collective-permute-start | bytes 786440 | tf_op jit(solution)/shard_map/while/body/eval_jaxpr/ppermute | solution.py:12
  23.4 1.7 copy-start
  23.5 1.7 copy-start.3
  23.5 18.3 %copy-start.6 = (bf16[128,2048]{1,0:T(8,128)(2,1)S(1)}, bf16[128,2048]{1,0:T(8,128)(2,1)}, u32[]{:S(2)}) copy-start(bf16[128,2048]{1,0:T(8,128)(2,1)} %get-tuple-element.382) | copy-start | bytes 1572868 | tf_op jit(solution)/shard_map/while
  25.2 16.7 %copy-start.4 = (bf16[128,2048]{1,0:T(8,128)(2,1)}, bf16[128,2048]{1,0:T(8,128)(2,1)S(1)}, u32[]{:S(2)}) copy-start(bf16[128,2048]{1,0:T(8,128)(2,1)S(1)} %select_dynamic-update-slice_fusion.6) | copy-start | bytes 1572868 | tf_op jit(solution)/shard_map/while
  41.9 0.8 copy-start.7
  42.7 11.5 %copy-start.2 = (bf16[256,2048]{1,0:T(8,128)(2,1)S(1)}, bf16[256,2048]{1,0:T(8,128)(2,1)}, u32[]{:S(2)}) copy-start(bf16[256,2048]{1,0:T(8,128)(2,1)} %get-tuple-element.402) | copy-start | bytes 3145732 | tf_op jit(solution)/shard_map/while
  42.7 11.5 %copy-start.8 = (s32[128]{0:T(128)S(1)}, s32[128]{0:T(128)}, u32[]{:S(2)}) copy-start(s32[128]{0:T(128)} %get-tuple-element.401) | copy-start | bytes 1540 | tf_op jit(solution)/shard_map/while
  48.9 5.3 %collective-permute-start = (bf16[64,2048]{1,0:T(8,128)(2,1)S(1)}, bf16[64,2048]{1,0:T(8,128)(2,1)S(1)}, u32[]{:S(2)}, u32[]{:S(2)}) collective-permute-start(bf16[64,2048]{1,0:T(8,128)(2,1)S(1)} %get-tuple-element.407), channel_id=1, source_target_pairs={{0,16},{1,17},{2,18},{3,19},{4,20},{5,21},{6,22},{7,23},{8,24},{9,... | collective-permute-start | bytes 786440 | tf_op jit(solution)/shard_map/while/body/eval_jaxpr/ppermute | solution.py:12
  54.5 18.3 %collective-permute-start.1 = (bf16[64,2048]{1,0:T(8,128)(2,1)S(1)}, bf16[64,2048]{1,0:T(8,128)(2,1)S(1)}, u32[]{:S(2)}, u32[]{:S(2)}) collective-permute-start(bf16[64,2048]{1,0:T(8,128)(2,1)S(1)} %get-tuple-element.351), channel_id=1, source_target_pairs={{16,0},{17,1},{18,2},{19,3},{20,4},{21,5},{22,6},{23,7},{24,8},{25... | collective-permute-start | bytes 786440 | tf_op jit(solution)/shard_map/while/body/eval_jaxpr/ppermute | solution.py:12
  55.8 3.4 copy-start
  55.8 3.4 copy-start.3
  55.8 17.0 %copy-start.6 = (bf16[128,2048]{1,0:T(8,128)(2,1)S(1)}, bf16[128,2048]{1,0:T(8,128)(2,1)}, u32[]{:S(2)}) copy-start(bf16[128,2048]{1,0:T(8,128)(2,1)} %get-tuple-element.382) | copy-start | bytes 1572868 | tf_op jit(solution)/shard_map/while
  59.2 13.7 %copy-start.4 = (bf16[128,2048]{1,0:T(8,128)(2,1)}, bf16[128,2048]{1,0:T(8,128)(2,1)S(1)}, u32[]{:S(2)}) copy-start(bf16[128,2048]{1,0:T(8,128)(2,1)S(1)} %select_dynamic-update-slice_fusion.6) | copy-start | bytes 1572868 | tf_op jit(solution)/shard_map/while
  72.9 0.8 copy-start.7
  73.7 1.0 copy-start.5
  73.8 317.7 %reduce-scatter.3.cloned.1.call-start = ((), (), s32[]{:S(2)}) async-start(), calls=%async_computation.2 | async-start | bytes 17825792 | tf_op jit(solution)/shard_map/reduce_scatter | solution.py:132
Sparse Core Ops, SparseCore 0:
  73.9 124.2 reduce-scatter.4
  202.8 188.5 reduce-scatter.2
where the time goes:
time: 404 us; the launch traced here: 401 us
  waiting for transfers between devices  346 us (86%)
  matrix products  20.5 us (5%)
  between operations  14.1 us (3%)
  other arithmetic  9.1 us (2%)
  starting transfers between devices  5.27 us (1%)
  local copies, waits for them, and re-layouts  4.91 us (1%)
    reduce_scatter x1, waiting for transfers between devices, local(): lax.psum_scatter(full_grad, 'batch', scatter_dimension=0, tiled=True)  192 us
    reduce_scatter x1, waiting for transfers between devices, local(): lax.psum_scatter(rel_total, ('hop', 'batch'), scatter_dimension=0, tiled=...  115 us
    ppermute x4, waiting for transfers between devices, from_behind(): return lax.ppermute(block, axis, route)  39.3 us
    dot_general x2, matrix products, lead(): lax.dot_general(block_rows, weight, (((1,), (1,)), ((), ())), preferred_e...  12.4 us
    dot_general x1, matrix products, local(): lax.dot_general(left_all, right_all, (((0,), (0,)), ((), ())), preferred_...  8.09 us
  transfers between devices with their start and end apart: 6, of which 6 were waited for; matrix products, arithmetic and copies ran while one was open for 4% of the time, Pallas kernels for 0%

commit v1 on v0

v1 whole, which is shorter than its diff:
```python
import jax
import jax.numpy as jnp
from jax import lax
from jax.sharding import PartitionSpec as P

F32 = jnp.float32
BF16 = jnp.bfloat16


def dot(a, b, ca, cb):
    return lax.dot_general(a, b, (((ca,), (cb,)), ((), ())), preferred_element_type=F32)


def split_sum(onehot, values):
    head = values.astype(BF16)
    rest = (values - head.astype(F32)).astype(BF16)
    return dot(onehot, head, 0, 0) + dot(onehot, rest, 0, 0)


def trail(query, cotangent, weight, table, ids):
    count_rel, width = table.shape
    half = width // 2
    onehot = (ids[:, None] == lax.iota(jnp.int32, count_rel)[None, :]).astype(BF16)
    rel = dot(onehot, table, 1, 0)
    r_re, r_im = rel[:, :half], rel[:, half:]
    qf = query.astype(F32)
    q_re, q_im = qf[:, :half], qf[:, half:]
    mixed = jnp.concatenate(
        [q_re * r_re - q_im * r_im, q_re * r_im + q_im * r_re], axis=1
    ).astype(BF16)
    pre = dot(mixed, weight, 1, 0)
    sig = jax.nn.sigmoid(pre)
    grad_pre = (cotangent.astype(F32) * (sig * (1.0 + pre * (1.0 - sig)))).astype(BF16)
    gz = dot(grad_pre, weight, 1, 1)
    gz_re, gz_im = gz[:, :half], gz[:, half:]
    grad_query = jnp.concatenate(
        [gz_re * r_re + gz_im * r_im, gz_im * r_re - gz_re * r_im], axis=1
    ).astype(BF16)
    grad_rel = jnp.concatenate([gz_re * q_re + gz_im * q_im, gz_im * q_re - gz_re * q_im], axis=1)
    return mixed, grad_pre, grad_query, split_sum(onehot, grad_rel).astype(BF16)


def local(section_rows, weights, relation_table, relation_ids):
    rows = section_rows[0]
    weight = weights[0]
    rows_dev, width = rows.shape
    count_rel = relation_table.shape[0]
    batch = lax.axis_size("batch")
    first = lax.axis_index("hop") == 0
    total_rows = rows_dev * batch
    zeros = jnp.zeros((rows_dev, width), BF16)

    query = lax.cond(first, lambda: dot(rows, weight, 1, 1).astype(BF16), lambda: zeros)
    received = lax.ppermute(query, "hop", [(0, 1)])
    mixed, grad_pre, grad_query, rel_part = lax.cond(
        first,
        lambda: (zeros, zeros, zeros, jnp.zeros((count_rel, width), BF16)),
        lambda: trail(received, rows, weight, relation_table, relation_ids),
    )
    right = jnp.where(first, rows, grad_pre)
    right_all = lax.all_gather(right, "batch", axis=0, tiled=True)

    half_rel = count_rel // 2
    query_back = lax.ppermute(grad_query, "hop", [(1, 0)])
    rel_back = lax.ppermute(rel_part[:half_rel], "hop", [(1, 0)])
    query_grad = jnp.where(first, query_back, grad_query)
    left = jnp.where(first, query_back, mixed)
    rel_own = jnp.where(first, rel_back, rel_part[half_rel:])

    cols = width // batch
    left_sent = left.reshape(rows_dev, batch, cols).transpose(1, 0, 2)
    left_cols = lax.all_to_all(left_sent, "batch", 0, 0, tiled=True).reshape(total_rows, cols)
    rel_rows = lax.all_to_all(
        rel_own.reshape(batch, half_rel // batch, width), "batch", 0, 0, tiled=True
    )
    relation_grad = jnp.sum(rel_rows.astype(F32), axis=0) * jnp.sqrt(F32(count_rel) / F32(total_rows))
    weight_grad = dot(left_cols, right_all, 0, 0) * (1.0 / jnp.sqrt(F32(total_rows)))
    return weight_grad[None], relation_grad, query_grad


def solution(mesh):
    return jax.shard_map(
        local,
        mesh=mesh,
        in_specs=(P("hop", "batch", None), P("hop", None, None), P(), P("batch")),
        out_specs=(P("hop", "batch", None), P(("hop", "batch"), None), P("batch", None)),
        check_vma=False,
    )
```

time: 404 us -> 166 us (0.41)
  the two profiles are of different devices: /device:TPU:9 before, /device:TPU:0 now
where the time goes in v1:
time: 166 us
  waiting for transfers between devices  111 us (67%)
  starting transfers between devices  15.6 us (9%)
  between operations  14.1 us (8%)
  matrix products  13.6 us (8%)
  local copies, waits for them, and re-layouts  6.16 us (4%)
  other arithmetic  4.65 us (3%)
    ppermute x1, waiting for transfers between devices, local(): query_back = lax.ppermute(grad_query, 'hop', [(1, 0)])  33.3 us
    all_gather x1, waiting for transfers between devices, local(): right_all = lax.all_gather(right, 'batch', axis=0, tiled=True)  28.2 us
    all_to_all x1, waiting for transfers between devices, local(): lax.all_to_all(rel_own.reshape(batch, half_rel // batch, width), 'batch',...  21.7 us
    all_to_all x1, waiting for transfers between devices, local(): lax.all_to_all(left_sent, 'batch', 0, 0, tiled=True)  15.1 us
    dot_general x2, matrix products, dot(): lax.dot_general(a, b, (((ca,), (cb,)), ((), ())), preferred_element_type=...  13.6 us
    ppermute x1, waiting for transfers between devices, local(): received = lax.ppermute(query, 'hop', [(0, 1)])  12 us
    all_to_all x1, starting transfers between devices, local(): lax.all_to_all(left_sent, 'batch', 0, 0, tiled=True)  6.85 us
    all_to_all x1, starting transfers between devices, local(): lax.all_to_all(rel_own.reshape(batch, half_rel // batch, width), 'batch',...  4.84 us
  transfers between devices with their start and end apart: 6, of which 6 were waited for; matrix products, arithmetic and copies ran while one was open for 4% of the time, Pallas kernels for 0%

profile of v1, /device:TPU:0, one launch (start us, length us, event | category | flops | bytes accessed | tf_op | source)
XLA Modules:
  0.0 165.5 jit_solution(1225597610352542905)
XLA Ops:
  7.2 0.0 copy-start
  7.2 0.0 copy-start.5
  7.2 0.0 all-gather.2.cloned.1.call-start
  7.2 1.4 copy.20
  8.6 6.3 %conditional.2 = (bf16[128,2048]{1,0:T(8,128)(2,1)S(1)}) conditional(s32[]{:T(128)} %convert_element_type.34, () %tuple.22, (bf16[128,2048]{0,1:T(8,128)(2,1)S(1)}, bf16[2048,2048]{1,0:T(8,128)(2,1)}) %tuple.54), branch_computations={%region_0.0_spmd, %region_1.0_spmd} | conditional | flops 1074003968 | bytes 9437192 | solution.py:53
  8.7 6.3 %convolution_convert_fusion = bf16[128,2048]{1,0:T(8,128)(2,1)S(1)} fusion(bf16[128,2048]{0,1:T(8,128)(2,1)S(1)} %get-tuple-element.49, bf16[2048,2048]{1,0:T(8,128)(2,1)} %get-tuple-element.18), kind=kOutput, calls=%fused_computation | convolution fusion | flops 1074003968 | bytes 9437184 | tf_op jit(solution)/shard_map/cond/branch_1_fun/dot_general | solution.py:11
  15.0 1.3 collective-permute-start
  16.3 12.0 %collective-permute-done = bf16[128,2048]{1,0:T(8,128)(2,1)S(1)} collective-permute-done((bf16[128,2048]{1,0:T(8,128)(2,1)S(1)}, bf16[128,2048]{1,0:T(8,128)(2,1)S(1)}, u32[]{:S(2)}, u32[]{:S(2)}) %collective-permute-start) | collective-permute-done | bytes 524320 | tf_op jit(solution)/shard_map/ppermute | solution.py:54
  28.3 0.0 copy-done
  28.3 0.0 copy-done.5
  28.3 1.1 conditional.3
  28.3 0.1 broadcast.6
  28.4 0.9 broadcast_in_dim.8.clone
  29.3 0.1 broadcast_in_dim.8.clone2
  29.4 0.1 broadcast_in_dim.8.clone2.1
  29.5 0.9 broadcast_select_fusion.1
  30.4 0.0 all-gather.2.cloned.1.call-update
  30.4 1.3 collective-permute-start.1
  31.7 0.5 copy.27
  32.3 1.3 collective-permute-start.2
  33.6 33.3 %collective-permute-done.1 = bf16[128,2048]{0,1:T(8,128)(2,1)S(1)} collective-permute-done((bf16[128,2048]{0,1:T(8,128)(2,1)}, bf16[128,2048]{0,1:T(8,128)(2,1)S(1)}, u32[]{:S(2)}, u32[]{:S(2)}) %collective-permute-start.1) | collective-permute-done | bytes 524320 | tf_op jit(solution)/shard_map/ppermute | solution.py:64
  66.9 0.0 copy-start.4
  66.9 0.8 copy-done.4
  67.7 1.9 %broadcast_select_fusion = (bf16[128,2048]{0,1:T(8,128)(2,1)S(1)}, bf16[128,2048]{0,1:T(8,128)(2,1)}) fusion(bf16[128,2048]{0,1:T(8,128)(2,1)} %copy-done.4, bf16[128,2048]{0,1:T(8,128)(2,1)} %get-tuple-element.59, pred[]{:T(512)S(6)} %eq.16, bf16[128,2048]{0,1:T(8,128)(2,1)S(1)} %get-tuple-element.60), kind=kLoop, calls=%fused_computation.32 | loop fusion | flops 524288 | bytes 2621441 | tf_op jit(solution)/shard_map/jit(_where)/select_n | solution.py:66
  69.6 6.8 %all-to-all-start = ((bf16[16,128,128]{1,2,0:T(8,128)(2,1)}), bf16[16,128,128]{1,2,0:T(8,128)(2,1)S(1)}, u32[]{:S(2)}, u32[]{:S(2)}) async-start(bf16[16,128,128]{1,2,0:T(8,128)(2,1)} %bitcast.3), calls=%async_computation | async-start | bytes 1048576 | tf_op jit(solution)/shard_map/all_to_all | solution.py:72
  76.5 1.0 collective-permute-done.2
  77.5 1.1 slice_select_fusion
  78.6 1.0 copy.29
  79.6 15.1 %all-to-all-done = bf16[16,128,128]{1,2,0:T(8,128)(2,1)S(1)} async-done(((bf16[16,128,128]{1,2,0:T(8,128)(2,1)}), bf16[16,128,128]{1,2,0:T(8,128)(2,1)S(1)}, u32[]{:S(2)}, u32[]{:S(2)}) %all-to-all-start) | async-done | bytes 524320 | tf_op jit(solution)/shard_map/all_to_all | solution.py:72
  94.6 4.8 %all-to-all-start.1 = ((bf16[16,8,2048]{2,1,0:T(8,128)(2,1)}), bf16[16,8,2048]{2,1,0:T(8,128)(2,1)S(1)}, u32[]{:S(2)}, u32[]{:S(2)}) async-start(bf16[16,8,2048]{2,1,0:T(8,128)(2,1)} %bitcast.6), calls=%async_computation.1 | async-start | bytes 1048576 | tf_op jit(solution)/shard_map/all_to_all | solution.py:73
  99.5 1.0 copy.31
  100.5 0.3 copy.25
  100.8 21.7 %all-to-all-done.1 = bf16[16,8,2048]{2,1,0:T(8,128)(2,1)S(1)} async-done(((bf16[16,8,2048]{2,1,0:T(8,128)(2,1)}), bf16[16,8,2048]{2,1,0:T(8,128)(2,1)S(1)}, u32[]{:S(2)}, u32[]{:S(2)}) %all-to-all-start.1) | async-done | bytes 524320 | tf_op jit(solution)/shard_map/all_to_all | solution.py:73
  122.5 0.1 convert_reduce_fusion
  122.6 0.6 broadcast_multiply_fusion
  123.2 28.2 %all-gather.2.cloned.1.call-done = bf16[2048,2048]{0,1:T(8,128)(2,1)} async-done(((bf16[128,2048]{0,1:T(8,128)(2,1)}), bf16[2048,2048]{0,1:T(8,128)(2,1)}) %all-gather.2.cloned.1.call-update) | async-done | bytes 8388624 | tf_op jit(solution)/shard_map/all_gather | solution.py:61
  151.4 7.3 %fusion.15 = f32[1,128,2048]{2,1,0:T(8,128)} fusion(bf16[2048,128]{1,0:T(8,128)(2,1)S(1)} %bitcast.21, bf16[2048,2048]{0,1:T(8,128)(2,1)} %all-gather.2.cloned.1.call-done), kind=kOutput, calls=%fused_computation.29 | convolution fusion | flops 1074003968 | bytes 9961472 | tf_op jit(solution)/shard_map/dot_general | solution.py:11
  (1 shorter events, 0.0 us)
Async XLA Ops:
  7.2 21.2 %copy-start = (bf16[256,2048]{1,0:T(8,128)(2,1)S(1)}, bf16[256,2048]{1,0:T(8,128)(2,1)}, u32[]{:S(2)}) copy-start(bf16[256,2048]{1,0:T(8,128)(2,1)} %param.10) | copy-start | bytes 3145732
  7.2 21.2 %copy-start.5 = (s32[128]{0:T(128)S(1)}, s32[128]{0:T(128)}, u32[]{:S(2)}) copy-start(s32[128]{0:T(128)} %param.11) | copy-start | bytes 1540
  7.2 144.2 %all-gather.2.cloned.1.call-start = ((), (), s32[]{:S(2)}) async-start(), calls=%async_computation.2 | async-start | bytes 8912896 | tf_op jit(solution)/shard_map/all_gather | solution.py:61
  15.0 13.4 %collective-permute-start = (bf16[128,2048]{1,0:T(8,128)(2,1)S(1)}, bf16[128,2048]{1,0:T(8,128)(2,1)S(1)}, u32[]{:S(2)}, u32[]{:S(2)}) collective-permute-start(bf16[128,2048]{1,0:T(8,128)(2,1)S(1)} %get-tuple-element.82), channel_id=1, source_target_pairs={{0,16},{1,17},{2,18},{3,19},{4,20},{5,21},{6,22},{7,23},{8,24},{9,... | collective-permute-start | bytes 1572872 | tf_op jit(solution)/shard_map/ppermute | solution.py:54
  30.4 36.5 %collective-permute-start.1 = (bf16[128,2048]{0,1:T(8,128)(2,1)}, bf16[128,2048]{0,1:T(8,128)(2,1)S(1)}, u32[]{:S(2)}, u32[]{:S(2)}) collective-permute-start(bf16[128,2048]{0,1:T(8,128)(2,1)} %get-tuple-element.59), channel_id=1, source_target_pairs={{16,0},{17,1},{18,2},{19,3},{20,4},{21,5},{22,6},{23,7},{24,8},{25... | collective-permute-start | bytes 1572872 | tf_op jit(solution)/shard_map/ppermute | solution.py:64
  32.3 45.2 %collective-permute-start.2 = (bf16[128,2048]{0,1:T(8,128)(2,1)S(1)}, bf16[128,2048]{0,1:T(8,128)(2,1)}, u32[]{:S(2)}, u32[]{:S(2)}) collective-permute-start(bf16[128,2048]{0,1:T(8,128)(2,1)S(1)} %slice.32), channel_id=1, source_target_pairs={{16,0},{17,1},{18,2},{19,3},{20,4},{21,5},{22,6},{23,7},{24,8},{25... | collective-permute-start | bytes 1572872 | tf_op jit(solution)/shard_map/ppermute | solution.py:65
  66.9 0.8 copy-start.4
  69.6 25.0 %all-to-all-start = ((bf16[16,128,128]{1,2,0:T(8,128)(2,1)}), bf16[16,128,128]{1,2,0:T(8,128)(2,1)S(1)}, u32[]{:S(2)}, u32[]{:S(2)}) async-start(bf16[16,128,128]{1,2,0:T(8,128)(2,1)} %bitcast.3), calls=%async_computation | async-start | bytes 1048576 | tf_op jit(solution)/shard_map/all_to_all | solution.py:72
  94.6 27.9 %all-to-all-start.1 = ((bf16[16,8,2048]{2,1,0:T(8,128)(2,1)}), bf16[16,8,2048]{2,1,0:T(8,128)(2,1)S(1)}, u32[]{:S(2)}, u32[]{:S(2)}) async-start(bf16[16,8,2048]{2,1,0:T(8,128)(2,1)} %bitcast.6), calls=%async_computation.1 | async-start | bytes 1048576 | tf_op jit(solution)/shard_map/all_to_all | solution.py:73
Sparse Core Ops, SparseCore 0:
  30.5 120.8 all-gather.1
